TPU v7x, 512 devices: a whole 4x4x16 slice. The times are simulated.
512 devices in a mesh: sec: 64 (over y, z), rad: 8 (over x, core).
Axes of the slice: x: 4, y: 4, z: 16, core: 2. Of those that a mesh axis runs over, the one named last changes fastest.
Arguments:
- transmembrane_potential: float32 [65536, 256], P(('sec', 'rad')), may hold values from -0.8 to -0.3
- channel_openness: float32 [3, 65536, 256], P(None, ('sec', 'rad')), may hold values from 0.02 to 0.95
- longitudinal_conductance: float32 [65536], P(('sec', 'rad')), may hold values from 0.05 to 0.4
- sector_map: int32 [65536, 1], P(('sec', 'rad')), may hold values from 0 to 63; in each aligned block of 128 rows (0 to 127, 128 to 255, ...) at most 4 rows name the same one
- cell_index: int32 [65536], P(('sec', 'rad')), may hold values from 0 to 255
- innervating_neuron: int32 [65536], P(('sec', 'rad')), may hold values from 0 to 511
- activation_moment: int32 [512], replicated, may hold values from 0 to 19
- synapse_position: int32 [65536], P(('sec', 'rad')), may hold values from 64 to 191
- radial_basis_matrix: float32 [256, 256], replicated, may hold values from -0.375 to 0.375
- spectrum: float32 [256, 512], P('sec'), may hold values from 1 to 20
Outputs:
- transmembrane_potential_later: float32 [65536, 256], P(('sec', 'rad'))
- channel_openness_later: float32 [3, 65536, 256], P(None, ('sec', 'rad'))
- potential: float32 [256, 256, 2, 512], P('sec', 'rad')
Inputs may be any that keep to these rules, and one draw needn't show every extreme that they name: `sector_map`: among the 128 fibres of one device, at most 4 lie in any one sector.
All inputs are finite; a program needn't handle non-finite values.
Results may differ from a plain program's by a relative error of at most 0.00007.
Values sent between devices are 32-bit elements; how exact they have to be, the bound alone decides.
A program may use at most 64 MiB of HBM per device.

v0:
```python
import math

import jax
import jax.numpy as jnp
from jax import lax
from jax.sharding import PartitionSpec as P

AZ = 512
RAD = 256
SUBSTEPS = 10


TIME_STEP = 0.005
G_SODIUM = 120.0
G_POTASSIUM = 36.0
G_LEAK = 0.3
E_SODIUM = 50.0
E_POTASSIUM = -77.0
E_LEAK = -54.4
APPLIED_AMPERES = 800.0


def sent_together(arrays, axis, split_dim, concat_dim, along):
    columns = [a.reshape(*a.shape[:along], -1) for a in arrays]
    both = jnp.concatenate(columns, axis=along)
    result, at, done = (
        lax.all_to_all(both, axis, split_axis=split_dim, concat_axis=concat_dim, tiled=True),
        0,
        [],
    )
    for a, column in zip(arrays, columns):
        share = result[..., at : at + column.shape[along]]
        done.append(share.reshape(*share.shape[:along], *a.shape[along:]))
        at += column.shape[along]
    return tuple(done)


def second_diff(values):
    left_side = jnp.concatenate([values[:, :1], values[:, :-1]], 1)
    right_side = jnp.concatenate([values[:, 1:], values[:, -1:]], 1)
    return left_side + right_side - 2.0 * values


def sarcolemma_model(
    transmembrane_potential,
    channel_openness,
    longitudinal_conductance,
    activation_substep_count,
    synapse_position,
):
    points = lax.broadcasted_iota(jnp.int32, transmembrane_potential.shape, 1)
    destination_position = (points == synapse_position[:, None]).astype(jnp.float32)

    def substep(present_substep_counter, state_pair):
        volt_now, gate_now = state_pair
        membrane_mv = 100.0 * volt_now
        ionic = (
            G_SODIUM * gate_now[0] ** 3 * gate_now[1] * (membrane_mv - E_SODIUM)
            + G_POTASSIUM * gate_now[2] ** 4 * (membrane_mv - E_POTASSIUM)
            + G_LEAK * (membrane_mv - E_LEAK)
        )
        activation_markers = (present_substep_counter >= activation_substep_count)[:, None].astype(
            jnp.float32
        )
        applied_excitation = APPLIED_AMPERES * destination_position * activation_markers
        opening = jnp.stack(
            [
                jax.nn.softplus((membrane_mv + 40.0) / 10.0),
                0.07 * jnp.exp(-(membrane_mv + 65.0) / 20.0),
                0.1 * jax.nn.softplus((membrane_mv + 55.0) / 10.0),
            ]
        )
        closing = jnp.stack(
            [
                4.0 * jnp.exp(-(membrane_mv + 65.0) / 18.0),
                jax.nn.sigmoid((membrane_mv + 35.0) / 10.0),
                0.125 * jnp.exp(-(membrane_mv + 65.0) / 80.0),
            ]
        )
        rate_sum = opening + closing
        steady = opening / rate_sum
        gate_after = steady + (gate_now - steady) * jnp.exp(-TIME_STEP * rate_sum)
        volt_after = (
            volt_now
            + longitudinal_conductance[:, None] * second_diff(volt_now)
            + TIME_STEP / 100.0 * (applied_excitation - ionic)
        )
        return (volt_after, gate_after)

    return lax.fori_loop(0, SUBSTEPS, substep, (transmembrane_potential, channel_openness))


def per_device(
    transmembrane_potential,
    channel_openness,
    longitudinal_conductance,
    sector_map,
    cell_index,
    innervating_neuron,
    activation_moment,
    synapse_position,
    radial_basis_matrix,
    spectrum,
):
    fibres, point_count = transmembrane_potential.shape
    unit_count = activation_moment.shape[0]
    unit_ids = lax.broadcasted_iota(jnp.int32, (fibres, unit_count), 1)
    activation_substep_count = jnp.sum(
        jnp.where(innervating_neuron[:, None] == unit_ids, activation_moment[None, :], 0), 1
    )
    transmembrane_potential_later, channel_openness_later = sarcolemma_model(
        transmembrane_potential,
        channel_openness,
        longitudinal_conductance,
        activation_substep_count,
        synapse_position,
    )
    source = longitudinal_conductance[:, None] * second_diff(transmembrane_potential_later)
    sectors = lax.axis_size("sec")
    band_count = lax.axis_size("rad")
    sector_width = AZ // sectors
    band_rows = RAD // band_count
    cell_count = sector_width * band_rows
    capacity = 2 * fibres // sectors
    slot_count = sectors * capacity
    chosen = sector_map[:, 0]
    member = (chosen[:, None] == lax.broadcasted_iota(jnp.int32, (fibres, sectors), 1)).astype(
        jnp.int32
    )
    slot_rank = jnp.sum(member * (jnp.cumsum(member, 0) - 1), 1)
    destination = chosen * capacity + slot_rank
    slot_ids = lax.broadcasted_iota(jnp.int32, (slot_count, fibres), 0)
    deposit_placement = (slot_ids == destination[None, :]).astype(jnp.float32)
    placed = jnp.dot(
        deposit_placement,
        source,
        precision=lax.Precision.HIGHEST,
        preferred_element_type=jnp.float32,
    )
    cell_code = cell_index % band_rows * sector_width + cell_index // band_rows + 1
    slot_codes = jnp.dot(
        deposit_placement,
        cell_code.astype(jnp.float32),
        precision=lax.Precision.HIGHEST,
        preferred_element_type=jnp.float32,
    )
    received, slot_codes = sent_together((placed, slot_codes), "sec", 0, 0, 1)
    cell_ids = lax.broadcasted_iota(jnp.int32, (slot_count, cell_count), 1)
    onehot = (slot_codes.astype(jnp.int32)[:, None] - 1 == cell_ids).astype(jnp.float32)
    cell_tile = lax.dot_general(
        received,
        onehot,
        (((0,), (0,)), ((), ())),
        precision=lax.Precision.HIGHEST,
        preferred_element_type=jnp.float32,
    )
    radial_field = lax.all_to_all(cell_tile, "rad", split_axis=0, concat_axis=1, tiled=True)
    radial_field = radial_field.reshape(radial_field.shape[0], RAD, sector_width)
    projected = jnp.einsum(
        "xra,rj->jxa", radial_field, radial_basis_matrix, precision=lax.Precision.HIGHEST
    )
    all_azimuths = lax.all_to_all(projected, "sec", split_axis=0, concat_axis=2, tiled=True)
    basis_local = all_azimuths.shape[0]
    slab_local = all_azimuths.shape[1]
    row_ids = lax.broadcasted_iota(jnp.int32, (AZ, AZ), 0)
    col_ids = lax.broadcasted_iota(jnp.int32, (AZ, AZ), 1)
    phase = (row_ids * col_ids % AZ).astype(jnp.float32) * (2.0 * math.pi / AZ)
    dft_table = jnp.concatenate([jnp.cos(phase), -jnp.sin(phase)], 1) * (1.0 / math.sqrt(AZ))
    flattened = all_azimuths.reshape(basis_local * slab_local, AZ)
    spectral = jnp.dot(
        flattened, dft_table, precision=lax.Precision.HIGHEST, preferred_element_type=jnp.float32
    )
    spectral = spectral.reshape(basis_local, slab_local, 2, AZ)
    potential = spectral * spectrum[:, None, None, :]
    return (transmembrane_potential_later, channel_openness_later, potential)


def solution(mesh):
    placed = (
        P(("sec", "rad"), None),
        P(None, ("sec", "rad"), None),
        P(("sec", "rad")),
        P(("sec", "rad"), None),
        P(("sec", "rad")),
        P(("sec", "rad")),
        P(),
        P(("sec", "rad")),
        P(),
        P("sec", None),
    )
    return jax.shard_map(
        per_device,
        mesh=mesh,
        in_specs=placed,
        out_specs=(
            P(("sec", "rad"), None),
            P(None, ("sec", "rad"), None),
            P("sec", "rad", None, None),
        ),
        check_vma=False,
    )
```

profile of v0, /device:TPU:1, one launch (start us, length us, event | category | flops | bytes accessed | tf_op | source)
XLA Modules:
  0.0 118.8 jit_solution(11665719003843973689)
XLA Ops:
  0.6 0.9 copy.62
  1.6 1.0 copy.63
  3.5 16.2 %while.18 = (s32[]{:T(128)}, f32[128,256]{1,0:T(8,128)S(1)}, f32[3,128,256]{2,1,0:T(8,128)S(1)}, f32[128]{0:T(128)}, s32[128]{0:T(128)S(1)}, /*index=5*/s32[128]{0:T(128)}, s32[]{:T(128)}) while((s32[]{:T(128)}, f32[128,256]{1,0:T(8,128)S(1)}, f32[3,128,256]{2,1,0:T(8,128)S(1)}, f32[128]{0:T(128)}, s32[128]{0:T(128)S(1)}, ...), condition=%wide.region_2.3_spmd.clone, body=%wide.region_1.2_spmd.clone.sunk | while | flops 2883842 | bytes 3803737 | solution.py:90
  3.7 1.1 fusion.82
  5.3 1.1 fusion.82
  6.9 1.1 fusion.82
  8.6 1.1 fusion.82
  10.2 1.1 fusion.82
  11.8 1.1 fusion.82
  13.4 1.1 fusion.82
  15.0 1.1 fusion.82
  16.7 1.1 fusion.82
  18.3 1.1 fusion.82
  20.6 1.0 fusion.32
  21.8 43.8 %all_to_all.40 = f32[64,4,257]{2,1,0:T(4,128)S(1)} all-to-all(f32[64,4,257]{2,1,0:T(4,128)S(1)} %pad_maximum_fusion.1), channel_id=1, replica_groups=mesh['sec'=64,'rad'=8] {'sec'}, dimensions={0} | all-to-all | bytes 526336 | tf_op jit(solution)/shard_map/all_to_all | solution.py:27
  66.4 13.2 %all_to_all.41 = f32[8,32,256]{2,1,0:T(8,128)S(1)} all-to-all(f32[8,32,256]{2,1,0:T(8,128)S(1)} %bitcast.61), channel_id=1, replica_groups=mesh['sec'=64,'rad'=8] {'rad'}, dimensions={0} | all-to-all | bytes 524288 | tf_op jit(solution)/shard_map/all_to_all | solution.py:157
  81.1 1.2 reshape.60
  82.3 6.5 %all-to-all-start.2 = ((f32[64,1,1024]{2,1,0:T(1,128)}), f32[64,1,1024]{2,1,0:T(1,128)S(1)}, u32[]{:S(2)}, u32[]{:S(2)}) async-start(f32[64,1,1024]{2,1,0:T(1,128)} %reshape.60), calls=%async_computation.2 | async-start | bytes 524288 | tf_op jit(solution)/shard_map/all_to_all | solution.py:162
  88.8 4.1 %sine_negate_fusion = (f32[512,512]{0,1:T(8,128)S(1)}, f32[512,512]{0,1:T(8,128)S(1)}) fusion(), kind=kLoop, calls=%fused_computation.42 | loop fusion | flops 3932160 | bytes 2097152 | tf_op jit(solution)/shard_map/neg | solution.py:168
  93.1 14.1 %all-to-all-done.2 = f32[64,1,1024]{2,1,0:T(1,128)S(1)} async-done(((f32[64,1,1024]{2,1,0:T(1,128)}), f32[64,1,1024]{2,1,0:T(1,128)S(1)}, u32[]{:S(2)}, u32[]{:S(2)}) %all-to-all-start.2) | async-done | bytes 262176 | tf_op jit(solution)/shard_map/all_to_all | solution.py:162
  107.8 1.9 %reduce.2 = f32[64,1024]{1,0:T(8,128)} reduce(f32[64,1,1024]{2,1,0:T(1,128)S(1)} %all-to-all-done.2, f32[]{:T(128)} %broadcast.401), dimensions={1}, to_apply=%all_to_all.34.reduce_sub_computation | reduce | bytes 524292 | tf_op jit(solution)/shard_map/all_to_all | solution.py:162
  109.7 1.3 %reshape.61 = f32[256,8,32]{2,1,0:T(8,128)S(1)} reshape(f32[64,1024]{1,0:T(8,128)} %reduce.2) | data formatting | bytes 524288
  111.0 6.7 %convolution_multiply_fusion = f32[4,32,2,512]{3,1,2,0:T(8,128)S(1)} fusion(f32[2,512,512,1]{2,1,0,3:T(8,128)S(1)} %bitcast.56, f32[4,32,64,8]{1,3,0,2:T(8,128)S(1)} %bitcast.57, f32[4,512]{1,0:T(4,128)S(1)} %copy-done.3), kind=kOutput, calls=%fused_computation.35 | convolution fusion | flops 805437440 | bytes 2891776 | tf_op jit(solution)/shard_map/dot_general | solution.py:170
  117.6 1.2 %copy.43 = f32[4,32,2,512]{3,2,1,0:T(2,128)} copy(f32[4,32,2,512]{3,1,2,0:T(8,128)S(1)} %convolution_multiply_fusion) | data formatting | bytes 1048576
  (71 shorter events, 9.9 us)
Async XLA Ops:
  0.6 79.7 %copy-start = (f32[256,256]{1,0:T(8,128)S(1)}, f32[256,256]{1,0:T(8,128)}, u32[]{:S(2)}) copy-start(f32[256,256]{1,0:T(8,128)} %param.20) | copy-start | bytes 786436
  3.5 16.5 %copy-start.4 = (s32[128,1]{0,1:T(1,128)S(1)}, s32[128,1]{0,1:T(1,128)}, u32[]{:S(2)}) copy-start(s32[128,1]{0,1:T(1,128)} %param.15) | copy-start | bytes 1540
  3.5 16.9 %copy-start.5 = (s32[128]{0:T(128)S(1)}, s32[128]{0:T(128)}, u32[]{:S(2)}) copy-start(s32[128]{0:T(128)} %param.16) | copy-start | bytes 1540
  19.7 46.1 %copy-start.1 = (f32[128,256]{1,0:T(8,128)}, f32[128,256]{1,0:T(8,128)S(1)}, u32[]{:S(2)}) copy-start(f32[128,256]{1,0:T(8,128)S(1)} %get-tuple-element.189) | copy-start | bytes 393220
  19.7 46.1 %copy-start.2 = (f32[3,128,256]{2,1,0:T(8,128)}, f32[3,128,256]{2,1,0:T(8,128)S(1)}, u32[]{:S(2)}) copy-start(f32[3,128,256]{2,1,0:T(8,128)S(1)} %get-tuple-element.190) | copy-start | bytes 1179652
  82.3 25.0 %all-to-all-start.2 = ((f32[64,1,1024]{2,1,0:T(1,128)}), f32[64,1,1024]{2,1,0:T(1,128)S(1)}, u32[]{:S(2)}, u32[]{:S(2)}) async-start(f32[64,1,1024]{2,1,0:T(1,128)} %reshape.60), calls=%async_computation.2 | async-start | bytes 524288 | tf_op jit(solution)/shard_map/all_to_all | solution.py:162
  92.9 18.1 %copy-start.3 = (f32[4,512]{1,0:T(4,128)S(1)}, f32[4,512]{1,0:T(4,128)}, u32[]{:S(2)}) copy-start(f32[4,512]{1,0:T(4,128)} %param.21) | copy-start | bytes 24580
where the time goes:
time: 121 us; the launch traced here: 119 us
  blocking collectives  57 us (47%)
  other arithmetic  21.9 us (18%)
  waiting for transfers between devices  14.1 us (12%)
  local copies, waits for them, and re-layouts  9.45 us (8%)
  matrix products  8.72 us (7%)
  starting transfers between devices  6.46 us (5%)
    all_to_all x1, blocking collectives, sent_together(): lax.all_to_all(both, axis, split_axis=split_dim, concat_axis=concat_dim,...  43.8 us
    all_to_all x1, waiting for transfers between devices, per_device(): lax.all_to_all(projected, 'sec', split_axis=0, concat_axis=2, tiled=True)  14.1 us
    all_to_all x1, blocking collectives, per_device(): lax.all_to_all(cell_tile, 'rad', split_axis=0, concat_axis=1, tiled=True)  13.2 us
    another operation x10, other arithmetic, substep(): jnp.stack([jax.nn.softplus((membrane_mv + 40.0) / 10.0), 0.07 * jnp.exp(-...  10.9 us
    dot_general x1, matrix products, per_device(): jnp.dot(flattened, dft_table, precision=lax.Precision.HIGHEST, preferred_...  6.67 us
    all_to_all x1, starting transfers between devices, per_device(): lax.all_to_all(projected, 'sec', split_axis=0, concat_axis=2, tiled=True)  6.46 us
    unnamed x17, local copies, waits for them, and re-layouts  5.63 us
    neg x1, other arithmetic, per_device(): -jnp.sin(phase)  4.12 us
  transfers between devices with their start and end apart: 1, of which 1 were waited for; matrix products, arithmetic and copies ran while one was open for 4% of the time, Pallas kernels for 0%

commit v1 on v0

v1 whole, which is shorter than its diff:
```python
import functools
import math

import jax
import jax.numpy as jnp
import numpy as np
from jax import lax
from jax.experimental import pallas as pl
from jax.experimental.pallas import tpu as pltpu
from jax.sharding import PartitionSpec as P

F32 = jnp.float32
BF16 = jnp.bfloat16
MESH = pl.DeviceIdType.MESH

AZ = 512
SUBSTEPS = 10
SEC = 64
RADN = 8
FIB = 128
ROWS = 32


def split2(x):
    hi = x.astype(BF16)
    return hi, (x - hi.astype(F32)).astype(BF16)


def split3(x):
    hi = x.astype(BF16)
    rest = x - hi.astype(F32)
    mid = rest.astype(BF16)
    return hi, mid, (rest - mid.astype(F32)).astype(BF16)


def mxu(a, b, dims=((1,), (0,))):
    return lax.dot_general(a, b, (dims, ((), ())), preferred_element_type=F32)


def iota(shape, dim):
    return lax.broadcasted_iota(jnp.int32, shape, dim)


def inverse(x):
    return pltpu.reciprocal(x, approx=True)


def membrane(k, v, m, h, n, left, right, cond, onset):
    e80 = jnp.exp(jnp.minimum(v * (-100.0 / 80.0) + (-65.0 / 80.0), 10.0))
    e40 = e80 * e80
    e20 = e40 * e40
    e10 = e20 * e20
    close_m = jnp.exp(v * (-100.0 / 18.0) + (-65.0 / 18.0 + math.log(4.0)))
    open_h = 0.07 * e20
    close_n = 0.125 * e80
    open_m = jnp.maximum(v * 10.0 + 4.0 + jnp.log(1.0 + e10 * math.exp(2.5)), 0.0)
    open_n = jnp.maximum(v + 0.55 + 0.1 * jnp.log(1.0 + e10 * math.exp(1.0)), 0.0)
    close_h = inverse(1.0 + e10 * math.exp(3.0))
    gates = []
    for gate, opening, closing in (
        (m, open_m, close_m),
        (h, open_h, close_h),
        (n, open_n, close_n),
    ):
        rate = opening + closing
        steady = opening * inverse(rate)
        gates.append(steady + (gate - steady) * jnp.exp(rate * -0.005))
    nn = n * n
    ionic = (
        (m * m * m * h) * (0.6 * v - 0.3)
        + (nn * nn) * (0.18 * v + 0.1386)
        + (0.0015 * v + 0.000816)
    )
    stimulus = jnp.where(onset <= float(k), 0.04, 0.0)
    after = v + cond * (left + right - 2.0 * v) + (stimulus - ionic)
    return [after] + gates


def neighbours(low, high, first, last):
    up_low, up_high = pltpu.roll(low, 1, 1), pltpu.roll(high, 1, 1)
    down_low, down_high = pltpu.roll(low, 127, 1), pltpu.roll(high, 127, 1)
    return (
        jnp.where(first, low, up_low),
        jnp.where(first, up_low, up_high),
        jnp.where(last, down_high, down_low),
        jnp.where(last, high, down_high),
    )


def exchange_kernel(
    v_hbm,
    gates_hbm,
    basis_hbm,
    cond_ref,
    sector_ref,
    cell_ref,
    neuron_ref,
    moment_ref,
    synapse_ref,
    v_out,
    gates_out,
    all_out,
    v_in,
    gates_in,
    basis,
    v_new,
    gates_new,
    cols,
    src,
    placed,
    got_fibres,
    big_hi,
    big_lo,
    slabs,
    field,
    projected,
    got_all,
    load_sem,
    basis_sem,
    store_sem,
    send_sem,
    local_sem,
    got_sem,
):
    me = lax.axis_index("sec")
    band = lax.axis_index("rad")

    loads = [
        pltpu.make_async_copy(v_hbm, v_in, load_sem.at[0]),
        pltpu.make_async_copy(gates_hbm, gates_in, load_sem.at[1]),
    ]
    for c in loads:
        c.start()
    load_basis = pltpu.make_async_copy(basis_hbm, basis, basis_sem)
    load_basis.start()

    barrier = pltpu.get_barrier_semaphore()

    def greet(i, carry):
        pl.semaphore_signal(
            barrier, inc=1, device_id={"sec": lax.rem(me + i, SEC)}, device_id_type=MESH
        )
        return carry

    lax.fori_loop(1, SEC, greet, 0)
    for i in range(1, RADN):
        pl.semaphore_signal(
            barrier, inc=1, device_id={"rad": lax.rem(band + i, RADN)}, device_id_type=MESH
        )

    sector_row = sector_ref[...].astype(F32)
    cell = cell_ref[...]
    azimuth = cell // 32
    code_row = ((azimuth % 4) * 64 + (azimuth // 4) * 32 + cell % 32 + 1).astype(F32)
    stacked = jnp.concatenate(
        [
            cond_ref[...],
            synapse_ref[...].astype(F32),
            neuron_ref[...].astype(F32),
            sector_row,
            code_row,
            jnp.zeros((123, FIB), F32),
        ],
        0,
    )
    as_cols = stacked.T
    unit = iota((FIB, 512), 1).astype(F32)
    moments = moment_ref[...].astype(F32)
    onset_col = jnp.sum(jnp.where(as_cols[:, 2:3] == unit, moments, 0.0), 1, keepdims=True)
    lane = iota((FIB, FIB), 1)
    cols[...] = jnp.where(lane == 2, onset_col, as_cols)
    same = (as_cols[:, 3:4] == sector_row) & (iota((FIB, FIB), 0) < lane)
    rank_row = jnp.sum(jnp.where(same, 1.0, 0.0), 0, keepdims=True)
    slot_row = sector_row * 8.0 + rank_row
    slot = iota((512, FIB), 0).astype(F32)
    into_slots = jnp.concatenate(
        [
            jnp.where(slot == slot_row, 1.0, 0.0).astype(BF16),
            jnp.where(slot == slot_row + 4.0, 1.0, 0.0).astype(BF16),
        ],
        1,
    )

    for c in loads:
        c.wait()

    def fibres(i, carry):
        rows = pl.ds(pl.multiple_of(i * ROWS, ROWS), ROWS)
        points = iota((ROWS, 128), 1)
        first, last = points == 0, points == 127
        info = cols[rows, :]
        cond = jnp.broadcast_to(info[:, 0:1], (ROWS, 128))
        synapse, onset = info[:, 1:2], info[:, 2:3]
        state, onsets = [], []
        for half in range(2):
            at = slice(128 * half, 128 * half + 128)
            state.append([v_in[rows, at]] + [gates_in[q, rows, at] for q in range(3)])
            onsets.append(
                jnp.where((points + 128 * half).astype(F32) == synapse, onset, 1e9)
            )
        for k in range(SUBSTEPS):
            l0, l1, r0, r1 = neighbours(state[0][0], state[1][0], first, last)
            state = [
                membrane(k, *state[0], l0, r0, cond, onsets[0]),
                membrane(k, *state[1], l1, r1, cond, onsets[1]),
            ]
        for half in range(2):
            at = slice(128 * half, 128 * half + 128)
            v_new[rows, at] = state[half][0]
            for q in range(3):
                gates_new[q, rows, at] = state[half][1 + q]
        l0, l1, r0, r1 = neighbours(state[0][0], state[1][0], first, last)
        src[rows, :] = cond * (l0 + r0 - 2.0 * state[0][0])
        high = cond * (l1 + r1 - 2.0 * state[1][0])
        src[pl.ds(pl.multiple_of(FIB + i * ROWS, ROWS), ROWS), :] = jnp.where(
            last, info[:, 4:5], high
        )
        return carry

    lax.fori_loop(0, FIB // ROWS, fibres, 0)

    stores = [
        pltpu.make_async_copy(v_new, v_out, store_sem.at[0]),
        pltpu.make_async_copy(gates_new, gates_out, store_sem.at[1]),
    ]
    for c in stores:
        c.start()

    s_hi, s_mid, s_lo = split3(src[...])
    placed[...] = mxu(into_slots, s_hi) + mxu(into_slots, s_mid) + mxu(into_slots, s_lo)

    pl.semaphore_wait(barrier, SEC + RADN - 2)

    def over_sectors(source, target, n):
        def send(i, carry):
            d = lax.rem(me + i, SEC)
            pltpu.make_async_remote_copy(
                source.at[pl.ds(pl.multiple_of(d * 8, 8), 8)],
                target.at[pl.ds(pl.multiple_of(me * 8, 8), 8)],
                send_sem.at[n],
                got_sem.at[n],
                device_id={"sec": d},
                device_id_type=MESH,
            ).start()
            return carry

        lax.fori_loop(1, SEC, send, 0)
        own = pl.ds(pl.multiple_of(me * 8, 8), 8)
        local = pltpu.make_async_copy(source.at[own], target.at[own], local_sem.at[n])
        local.start()
        return local

    def all_of(buffer, sem):
        pltpu.make_async_copy(buffer, buffer, sem).wait()

    local1 = over_sectors(placed, got_fibres, 0)

    load_basis.wait()
    b_hi, b_lo = split2(basis[...])
    row, col = iota((512, 256), 0), iota((512, 256), 1)
    for half in range(2):
        pick = jnp.where(
            ((row // 8) * 4 + row % 4 == col) & ((row % 8) // 4 == half), 1.0, 0.0
        ).astype(BF16)
        at = slice(256 * half, 256 * half + 256)
        big_hi[:, at] = mxu(pick, b_hi, ((1,), (1,))).astype(BF16)
        big_lo[:, at] = mxu(pick, b_lo, ((1,), (1,))).astype(BF16)

    most = pl.ds(0, 8 * (SEC - 1))
    all_of(got_fibres.at[most], got_sem.at[0])
    local1.wait()

    x = got_fibres[...]
    end = iota((8, 128), 1) == 127
    codes = mxu(jnp.where(end, 1.0, 0.0).astype(BF16), x.astype(BF16), ((1,), (1,)))
    slots = iota((8, 512), 1)
    upper = slots % 8 >= 4
    codes = jnp.where(upper, codes + 256.0, pltpu.roll(codes, 508, 1)) - 1.0
    into_cells = jnp.where(iota((512, 512), 0).astype(F32) == codes[0:1], 1.0, 0.0).astype(BF16)
    rows8 = iota((512, 128), 0) % 8
    coded = (rows8 >= 4) & (iota((512, 128), 1) == 127)
    x = jnp.where(coded, 0.0, x)
    sums = jnp.sum(x, 1, keepdims=True)
    sums = sums + pltpu.roll(jnp.broadcast_to(sums, (512, 128)), 4, 0)
    x = jnp.where(coded, -sums, x)
    x_hi, x_lo = split2(x)
    cells = mxu(into_cells, x_hi) + mxu(into_cells, x_lo)

    lanes = iota((64, 128), 1)
    wide, odd = lanes >= 64, lanes % 64 >= 32
    for half in range(2):
        t = [cells[256 * half + 64 * a : 256 * half + 64 * a + 64] for a in range(4)]
        for a in range(2):
            p, q = t[a], t[a + 2]
            t[a] = jnp.where(wide, pltpu.roll(q, 64, 1), p)
            t[a + 2] = jnp.where(wide, q, pltpu.roll(p, 64, 1))
        for a in (0, 2):
            p, q = t[a], t[a + 1]
            t[a] = jnp.where(odd, pltpu.roll(q, 32, 1), p)
            t[a + 1] = jnp.where(odd, q, pltpu.roll(p, 96, 1))
        for b in range(4):
            slabs[4 * half + b] = t[b].reshape(2, 32, 128)

    for i in range(1, RADN):
        d = lax.rem(band + i, RADN)
        pltpu.make_async_remote_copy(
            slabs.at[d],
            field.at[:, band],
            send_sem.at[1],
            got_sem.at[1],
            device_id={"rad": d},
            device_id_type=MESH,
        ).start()
    local2 = pltpu.make_async_copy(slabs.at[band], field.at[:, band], local_sem.at[1])
    local2.start()
    all_of(field.at[:, pl.ds(0, RADN - 1)], got_sem.at[1])
    local2.wait()

    f_hi, f_lo = split2(field[...].reshape(512, 128))
    projected[...] = mxu(big_hi[...], f_hi) + mxu(big_hi[...], f_lo) + mxu(big_lo[...], f_hi)
    local3 = over_sectors(projected, got_all, 2)
    for c in stores:
        c.wait()
    all_of(placed.at[most], send_sem.at[0])
    all_of(slabs.at[pl.ds(0, RADN - 1)], send_sem.at[1])
    all_of(got_all.at[most], got_sem.at[2])
    local3.wait()
    all_out[...] = got_all[...]
    all_of(projected.at[most], send_sem.at[2])


def spectral_kernel(
    all_ref, table_hi, table_lo, spectrum_ref, v_hbm, gates_hbm, out_ref, v_out, gates_out, sem
):
    passed = [
        pltpu.make_async_copy(v_hbm, v_out, sem.at[0]),
        pltpu.make_async_copy(gates_hbm, gates_out, sem.at[1]),
    ]
    for c in passed:
        c.start()
    parts = []
    for j in range(4):
        z = all_ref[pl.ds(j, 128, stride=4), :].T
        parts.append(jnp.concatenate([z[32 * a : 32 * a + 32] for a in range(4)], 1))
    hi, lo = split2(jnp.concatenate(parts, 0))
    for tile in range(4):
        at = slice(128 * tile, 128 * tile + 128)
        scale = jnp.concatenate(
            [jnp.broadcast_to(spectrum_ref[j : j + 1, at], (32, 128)) for j in range(4)], 0
        )
        for part in range(2):
            to = slice(512 * part + 128 * tile, 512 * part + 128 * tile + 128)
            y = mxu(hi, table_hi[:, to]) + mxu(lo, table_hi[:, to]) + mxu(hi, table_lo[:, to])
            out_ref[pl.ds(2 * tile + part, 128, stride=8), :] = y * scale
    for c in passed:
        c.wait()


def azimuth_table():
    low, rest = np.meshgrid(np.arange(4), np.arange(128), indexing="ij")
    azimuth = (rest * 4 + low).reshape(-1)
    phase = (azimuth[:, None] * np.arange(AZ)[None, :] % AZ) * (2.0 * math.pi / AZ)
    table = np.concatenate([np.cos(phase), -np.sin(phase)], 1) / math.sqrt(AZ)
    hi = table.astype(np.float32).astype(jnp.bfloat16)
    lo = (table - hi.astype(np.float64)).astype(np.float32).astype(jnp.bfloat16)
    return hi, lo


def per_device(
    voltage,
    gates,
    conductance,
    sector_map,
    cell_index,
    neuron,
    moment,
    synapse,
    basis,
    spectrum,
):
    any_space = pl.BlockSpec(memory_space=pl.ANY)
    vmem = pl.BlockSpec(memory_space=pltpu.VMEM)
    v_later, gates_later, everything = pl.pallas_call(
        exchange_kernel,
        out_shape=[
            jax.ShapeDtypeStruct((FIB, 256), F32),
            jax.ShapeDtypeStruct((3, FIB, 256), F32),
            jax.ShapeDtypeStruct((512, 128), F32),
        ],
        in_specs=[any_space] * 3 + [vmem] * 6,
        out_specs=[any_space, any_space, vmem],
        scratch_shapes=[
            pltpu.VMEM((FIB, 256), F32),
            pltpu.VMEM((3, FIB, 256), F32),
            pltpu.VMEM((256, 256), F32),
            pltpu.VMEM((FIB, 256), F32),
            pltpu.VMEM((3, FIB, 256), F32),
            pltpu.VMEM((FIB, 128), F32),
            pltpu.VMEM((2 * FIB, 128), F32),
            pltpu.VMEM((512, 128), F32),
            pltpu.VMEM((512, 128), F32),
            pltpu.VMEM((512, 512), BF16),
            pltpu.VMEM((512, 512), BF16),
            pltpu.VMEM((8, 2, 32, 128), F32),
            pltpu.VMEM((2, 8, 32, 128), F32),
            pltpu.VMEM((512, 128), F32),
            pltpu.VMEM((512, 128), F32),
            pltpu.SemaphoreType.DMA((2,)),
            pltpu.SemaphoreType.DMA,
            pltpu.SemaphoreType.DMA((2,)),
            pltpu.SemaphoreType.DMA((3,)),
            pltpu.SemaphoreType.DMA((3,)),
            pltpu.SemaphoreType.DMA((3,)),
        ],
        compiler_params=pltpu.CompilerParams(
            collective_id=0, has_side_effects=True, vmem_limit_bytes=32 << 20
        ),
    )(
        voltage,
        gates,
        basis,
        conductance.reshape(1, FIB),
        sector_map.reshape(1, FIB),
        cell_index.reshape(1, FIB),
        neuron.reshape(1, FIB),
        moment.reshape(1, 512),
        synapse.reshape(1, FIB),
    )
    table_hi, table_lo = azimuth_table()
    tiles, v_final, gates_final = pl.pallas_call(
        spectral_kernel,
        out_shape=[
            jax.ShapeDtypeStruct((1024, 128), F32),
            jax.ShapeDtypeStruct((FIB, 256), F32),
            jax.ShapeDtypeStruct((3, FIB, 256), F32),
        ],
        in_specs=[vmem] * 4 + [any_space] * 2,
        out_specs=[vmem, any_space, any_space],
        scratch_shapes=[pltpu.SemaphoreType.DMA((2,))],
        compiler_params=pltpu.CompilerParams(vmem_limit_bytes=32 << 20),
    )(
        everything,
        jnp.asarray(table_hi),
        jnp.asarray(table_lo),
        spectrum,
        v_later,
        gates_later,
    )
    potential = tiles.reshape(4, 32, 4, 2, 128).transpose(0, 1, 3, 2, 4).reshape(4, 32, 2, AZ)
    return v_final, gates_final, potential


def solution(mesh):
    placed = (
        P(("sec", "rad"), None),
        P(None, ("sec", "rad"), None),
        P(("sec", "rad")),
        P(("sec", "rad"), None),
        P(("sec", "rad")),
        P(("sec", "rad")),
        P(),
        P(("sec", "rad")),
        P(),
        P("sec", None),
    )
    return jax.shard_map(
        per_device,
        mesh=mesh,
        in_specs=placed,
        out_specs=(
            P(("sec", "rad"), None),
            P(None, ("sec", "rad"), None),
            P("sec", "rad", None, None),
        ),
        check_vma=False,
    )
```

time: 121 us -> 68.8 us (0.57); the launches traced: 119 us -> 68.5 us
  Pallas kernels: 0 us -> 61.8 us
  blocking collectives: 57 us -> 0 us
  other arithmetic: 21.9 us -> 0 us
  waiting for transfers between devices: 14.1 us -> 0 us
  matrix products: 8.72 us -> 0 us
  starting transfers between devices: 6.46 us -> 0 us
  local copies, waits for them, and re-layouts: 9.45 us -> 5.98 us
    pallas_call x0 -> x2, Pallas kernels: none -> 61.8 us  [the longest x1 59.9 us: per_device(): pl.pallas_call(exchange_kernel, out_shape=[jax.ShapeDtypeStruct((FIB, 256...]
    all_to_all x2 -> x0, blocking collectives: 57 us -> none  [the longest x1 43.8 us: sent_together(): lax.all_to_all(both, axis, split_axis=split_dim, concat_axis=concat_dim,...]
    all_to_all x1 -> x0, waiting for transfers between devices: 14.1 us -> none  [per_device(): lax.all_to_all(projected, 'sec', split_axis=0, concat_axis=2, tiled=True)]
    another operation x11 -> x0, other arithmetic: 11 us -> none  [the longest x10 10.9 us: substep(): jnp.stack([jax.nn.softplus((membrane_mv + 40.0) / 10.0), 0.07 * jnp.exp(-...]
    dot_general x5 -> x0, matrix products: 8.72 us -> none  [the longest x1 6.67 us: per_device(): jnp.dot(flattened, dft_table, precision=lax.Precision.HIGHEST, preferred_...]
    all_to_all x1 -> x0, starting transfers between devices: 6.46 us -> none  [per_device(): lax.all_to_all(projected, 'sec', split_axis=0, concat_axis=2, tiled=True)]
    neg x1 -> x0, other arithmetic: 4.12 us -> none  [per_device(): -jnp.sin(phase)]
    add x11 -> x0, other arithmetic: 3.22 us -> none  [the longest x10 3.22 us: substep(): gate_after = steady + (gate_now - steady) * jnp.exp(-TIME_STEP * rate_sum)]
  transfers between devices with their start and end apart: 1 -> 0, of which waited for: 1 -> 0; matrix products, arithmetic and copies ran while one was open for 4% -> 0% of each run, Pallas kernels for 0% -> 0%
where the time goes in v1:
time: 68.8 us; the launch traced here: 68.5 us
  Pallas kernels  61.8 us (90%)
  local copies, waits for them, and re-layouts  5.98 us (9%)
  between operations  0.71 us (1%)
    pallas_call x1, Pallas kernels, per_device(): pl.pallas_call(exchange_kernel, out_shape=[jax.ShapeDtypeStruct((FIB, 256...  59.9 us
    unnamed x24, local copies, waits for them, and re-layouts  5.98 us
    pallas_call x1, Pallas kernels, per_device(): pl.pallas_call(spectral_kernel, out_shape=[jax.ShapeDtypeStruct((1024, 12...  1.88 us

profile of v1, /device:TPU:1, one launch (start us, length us, event | category | flops | bytes accessed | tf_op | source)
XLA Modules:
  0.0 68.5 jit_solution(4500424690799754109)
XLA Ops:
  0.6 0.0 copy-start.10
  0.6 0.0 copy-start.11
  0.7 0.0 copy-start.6
  0.7 0.0 copy-start.7
  0.7 0.0 copy-start.8
  0.7 0.0 copy-start.9
  0.7 0.6 copy-done.10
  1.3 0.0 copy-done.11
  1.3 0.0 copy-done.6
  1.3 0.0 copy-done.7
  1.4 0.0 copy-done.8
  1.4 0.0 copy-done.9
  1.4 0.0 copy-start.2
  1.4 1.0 %copy-done.2 = f32[3,128,256]{2,1,0:T(8,128)S(1)} copy-done((f32[3,128,256]{2,1,0:T(8,128)S(1)}, f32[3,128,256]{2,1,0:T(8,128)}, u32[]{:S(2)}) %copy-start.2) | copy-done | bytes 393240
  2.4 0.0 copy-start.3
  2.4 0.9 %copy-done.3 = f32[256,256]{1,0:T(8,128)S(1)} copy-done((f32[256,256]{1,0:T(8,128)S(1)}, f32[256,256]{1,0:T(8,128)}, u32[]{:S(2)}) %copy-start.3) | copy-done | bytes 262168
  3.3 0.0 copy-start.4
  3.3 0.9 %copy-done.4 = f32[128,256]{1,0:T(8,128)S(1)} copy-done((f32[128,256]{1,0:T(8,128)S(1)}, f32[128,256]{1,0:T(8,128)}, u32[]{:S(2)}) %copy-start.4) | copy-done | bytes 131096
  4.2 59.9 %shard_map.139 = (f32[128,256]{1,0:T(8,128)S(1)}, f32[3,128,256]{2,1,0:T(8,128)S(1)}, f32[512,128]{1,0:T(8,128)S(1)}) custom-call(f32[128,256]{1,0:T(8,128)S(1)} %copy-done.4, f32[3,128,256]{2,1,0:T(8,128)S(1)} %copy-done.2, f32[256,256]{1,0:T(8,128)S(1)} %copy-done.3, f32[1,128]{1,0:T(1,128)S(1)} %bitcast.12, s32[1,128]{1,0:T(1,128)S(1)} %bitcast.13, ...), custom_call_target="tpu_custom_call" | custom-call | tf_op jit(solution)/shard_map/pallas_call | solution.py:383
  64.1 0.0 copy-done.5
  64.1 0.0 copy-start
  64.1 1.2 %copy-done = bf16[512,1024]{1,0:T(8,128)(2,1)S(1)} copy-done((bf16[512,1024]{1,0:T(8,128)(2,1)S(1)}, bf16[512,1024]{1,0:T(8,128)(2,1)}, u32[]{:S(2)}) %copy-start) | copy-done | bytes 1048600
  65.4 1.2 %copy-done.1 = bf16[512,1024]{1,0:T(8,128)(2,1)S(1)} copy-done((bf16[512,1024]{1,0:T(8,128)(2,1)S(1)}, bf16[512,1024]{1,0:T(8,128)(2,1)}, u32[]{:S(2)}) %copy-start.1) | copy-done | bytes 1048600
  66.6 1.9 %shard_map.140 = (f32[1024,128]{1,0:T(8,128)}, f32[128,256]{1,0:T(8,128)}, f32[3,128,256]{2,1,0:T(8,128)}) custom-call(f32[512,128]{1,0:T(8,128)S(1)} %get-tuple-element.9.all_ref, bf16[512,1024]{1,0:T(8,128)(2,1)S(1)} %copy-done.1, bf16[512,1024]{1,0:T(8,128)(2,1)S(1)} %copy-done, f32[4,512]{1,0:T(4,128)S(1)} %copy-done.5, ...), custom_call_target="tpu_custom_call" | custom-call | tf_op jit(solution)/shard_map/pallas_call | solution.py:430
  (2 shorter events, 0.0 us)
Async XLA Ops:
  0.6 0.7 copy-start.10
  0.6 0.7 copy-start.11
  0.7 0.7 %copy-start.6 = (s32[512]{0:T(512)S(1)}, s32[512]{0:T(512)}, u32[]{:S(2)}) copy-start(s32[512]{0:T(512)} %param.18) | copy-start | bytes 6148
  0.7 0.7 %copy-start.7 = (f32[128]{0:T(128)S(1)}, f32[128]{0:T(128)}, u32[]{:S(2)}) copy-start(f32[128]{0:T(128)} %param.14) | copy-start | bytes 1540
  0.7 0.7 copy-start.8
  0.7 0.7 %copy-start.9 = (s32[128]{0:T(128)S(1)}, s32[128]{0:T(128)}, u32[]{:S(2)}) copy-start(s32[128]{0:T(128)} %param.16) | copy-start | bytes 1540
  1.4 1.0 %copy-start.2 = (f32[3,128,256]{2,1,0:T(8,128)S(1)}, f32[3,128,256]{2,1,0:T(8,128)}, u32[]{:S(2)}) copy-start(f32[3,128,256]{2,1,0:T(8,128)} %gates_hbm.1) | copy-start | bytes 1179652
  2.4 0.9 %copy-start.3 = (f32[256,256]{1,0:T(8,128)S(1)}, f32[256,256]{1,0:T(8,128)}, u32[]{:S(2)}) copy-start(f32[256,256]{1,0:T(8,128)} %basis_hbm.1) | copy-start | bytes 786436
  3.3 0.9 %copy-start.4 = (f32[128,256]{1,0:T(8,128)S(1)}, f32[128,256]{1,0:T(8,128)}, u32[]{:S(2)}) copy-start(f32[128,256]{1,0:T(8,128)} %v_hbm.1) | copy-start | bytes 393220
  4.2 59.9 %copy-start.5 = (f32[4,512]{1,0:T(4,128)S(1)}, f32[4,512]{1,0:T(4,128)}, u32[]{:S(2)}) copy-start(f32[4,512]{1,0:T(4,128)} %spectrum_ref.1) | copy-start | bytes 24580
  64.1 1.2 %copy-start = (bf16[512,1024]{1,0:T(8,128)(2,1)S(1)}, bf16[512,1024]{1,0:T(8,128)(2,1)}, u32[]{:S(2)}) copy-start(bf16[512,1024]{1,0:T(8,128)(2,1)} %constant.5.clone.table_lo) | copy-start | bytes 3145732
  65.4 1.2 %copy-start.1 = (bf16[512,1024]{1,0:T(8,128)(2,1)S(1)}, bf16[512,1024]{1,0:T(8,128)(2,1)}, u32[]{:S(2)}) copy-start(bf16[512,1024]{1,0:T(8,128)(2,1)} %constant.4.clone.table_hi) | copy-start | bytes 3145732

commit v2 on v1

--- a/solution.py
+++ b/solution.py
@@ -91,31 +91,38 @@
     v_hbm,
     gates_hbm,
     basis_hbm,
+    cond_hbm,
+    sector_hbm,
+    cell_hbm,
+    neuron_hbm,
+    moment_hbm,
+    synapse_hbm,
+    v_out,
+    gates_out,
+    all_out,
+    v_in,
+    gates_in,
+    basis,
     cond_ref,
     sector_ref,
     cell_ref,
     neuron_ref,
     moment_ref,
     synapse_ref,
-    v_out,
-    gates_out,
-    all_out,
-    v_in,
-    gates_in,
-    basis,
     v_new,
     gates_new,
     cols,
     src,
+    codes_out,
+    codes_in,
     placed,
     got_fibres,
-    big_hi,
-    big_lo,
     slabs,
     field,
     projected,
     got_all,
     load_sem,
+    small_sem,
     basis_sem,
     store_sem,
     send_sem,
@@ -131,6 +138,21 @@
     ]
     for c in loads:
         c.start()
+    small = [
+        pltpu.make_async_copy(a, b, small_sem.at[i])
+        for i, (a, b) in enumerate(
+            [
+                (cond_hbm, cond_ref),
+                (sector_hbm, sector_ref),
+                (cell_hbm, cell_ref),
+                (neuron_hbm, neuron_ref),
+                (moment_hbm, moment_ref),
+                (synapse_hbm, synapse_ref),
+            ]
+        )
+    ]
+    for c in small:
+        c.start()
     load_basis = pltpu.make_async_copy(basis_hbm, basis, basis_sem)
     load_basis.start()
 
@@ -148,17 +170,16 @@
             barrier, inc=1, device_id={"rad": lax.rem(band + i, RADN)}, device_id_type=MESH
         )
 
+    for c in small:
+        c.wait()
     sector_row = sector_ref[...].astype(F32)
-    cell = cell_ref[...]
-    azimuth = cell // 32
-    code_row = ((azimuth % 4) * 64 + (azimuth // 4) * 32 + cell % 32 + 1).astype(F32)
     stacked = jnp.concatenate(
         [
             cond_ref[...],
             synapse_ref[...].astype(F32),
             neuron_ref[...].astype(F32),
             sector_row,
-            code_row,
+            cell_ref[...].astype(F32),
             jnp.zeros((123, FIB), F32),
         ],
         0,
@@ -167,18 +188,17 @@
     unit = iota((FIB, 512), 1).astype(F32)
     moments = moment_ref[...].astype(F32)
     onset_col = jnp.sum(jnp.where(as_cols[:, 2:3] == unit, moments, 0.0), 1, keepdims=True)
-    lane = iota((FIB, FIB), 1)
+    line, lane = iota((FIB, FIB), 0), iota((FIB, FIB), 1)
     cols[...] = jnp.where(lane == 2, onset_col, as_cols)
-    same = (as_cols[:, 3:4] == sector_row) & (iota((FIB, FIB), 0) < lane)
-    rank_row = jnp.sum(jnp.where(same, 1.0, 0.0), 0, keepdims=True)
-    slot_row = sector_row * 8.0 + rank_row
-    slot = iota((512, FIB), 0).astype(F32)
-    into_slots = jnp.concatenate(
-        [
-            jnp.where(slot == slot_row, 1.0, 0.0).astype(BF16),
-            jnp.where(slot == slot_row + 4.0, 1.0, 0.0).astype(BF16),
-        ],
-        1,
+    same = as_cols[:, 3:4] == sector_row
+    rank_row = jnp.sum(jnp.where(same & (line < lane), 1.0, 0.0), 0, keepdims=True)
+    rank_col = jnp.sum(jnp.where(same & (lane < line), 1.0, 0.0), 1, keepdims=True)
+    slot = iota((256, FIB), 0).astype(F32)
+    into_slots = jnp.where(slot == sector_row * 4.0 + rank_row, 1.0, 0.0).astype(BF16)
+    into_sectors = jnp.where(iota((SEC, FIB), 0).astype(F32) == sector_row, 1.0, 0.0)
+    at_lane = (lane - 4 * lax.rem(me, 32)).astype(F32) == rank_col
+    codes_out[...] = mxu(
+        into_sectors.astype(BF16), jnp.where(at_lane, as_cols[:, 4:5] + 1.0, 0.0).astype(BF16)
     )
 
     for c in loads:
@@ -210,11 +230,11 @@
             for q in range(3):
                 gates_new[q, rows, at] = state[half][1 + q]
         l0, l1, r0, r1 = neighbours(state[0][0], state[1][0], first, last)
-        src[rows, :] = cond * (l0 + r0 - 2.0 * state[0][0])
+        low = cond * (l0 + r0 - 2.0 * state[0][0])
         high = cond * (l1 + r1 - 2.0 * state[1][0])
-        src[pl.ds(pl.multiple_of(FIB + i * ROWS, ROWS), ROWS), :] = jnp.where(
-            last, info[:, 4:5], high
-        )
+        even = points % 32 < 16
+        src[0, rows, :] = jnp.where(even, low, pltpu.roll(high, 16, 1))
+        src[1, rows, :] = jnp.where(even, pltpu.roll(low, 112, 1), high)
         return carry
 
     lax.fori_loop(0, FIB // ROWS, fibres, 0)
@@ -226,26 +246,38 @@
     for c in stores:
         c.start()
 
-    s_hi, s_mid, s_lo = split3(src[...])
-    placed[...] = mxu(into_slots, s_hi) + mxu(into_slots, s_mid) + mxu(into_slots, s_lo)
+    for c in range(2):
+        s_hi, s_mid, s_lo = split3(src[c])
+        placed[c] = mxu(into_slots, s_hi) + mxu(into_slots, s_mid) + mxu(into_slots, s_lo)
 
     pl.semaphore_wait(barrier, SEC + RADN - 2)
 
-    def over_sectors(source, target, n):
-        def send(i, carry):
-            d = lax.rem(me + i, SEC)
+    y, z = me // 16, lax.rem(me, 16)
+
+    def over_sectors(source, target, n, rows):
+        own = pl.ds(pl.multiple_of(me * rows, rows), rows)
+
+        def send(to_y, to_z):
+            d = lax.rem(y + to_y, 4) * 16 + lax.rem(z + to_z, 16)
             pltpu.make_async_remote_copy(
-                source.at[pl.ds(pl.multiple_of(d * 8, 8), 8)],
-                target.at[pl.ds(pl.multiple_of(me * 8, 8), 8)],
+                source.at[pl.ds(pl.multiple_of(d * rows, rows), rows)],
+                target.at[own],
                 send_sem.at[n],
                 got_sem.at[n],
                 device_id={"sec": d},
                 device_id_type=MESH,
             ).start()
+
+        def send_far(i, carry):
+            away = 8 - (i + 1) // 2
+            to_z = jnp.where(lax.rem(i, 2) == 1, away, 16 - away)
+            for to_y in (2, 1, 3, 0):
+                send(to_y, to_z)
             return carry
 
-        lax.fori_loop(1, SEC, send, 0)
-        own = pl.ds(pl.multiple_of(me * 8, 8), 8)
+        lax.fori_loop(0, 15, send_far, 0)
+        for to_y in (2, 1, 3):
+            send(to_y, 0)
         local = pltpu.make_async_copy(source.at[own], target.at[own], local_sem.at[n])
         local.start()
         return local
@@ -253,80 +285,82 @@
     def all_of(buffer, sem):
         pltpu.make_async_copy(buffer, buffer, sem).wait()
 
-    local1 = over_sectors(placed, got_fibres, 0)
+    most = pl.ds(0, SEC - 1)
+    most4 = pl.ds(0, 4 * (SEC - 1))
+    local_codes = over_sectors(codes_out, codes_in, 0, 1)
+    local_fibres = [
+        over_sectors(placed.at[c], got_fibres.at[c], 1 + c, 4) for c in range(2)
+    ]
 
     load_basis.wait()
-    b_hi, b_lo = split2(basis[...])
-    row, col = iota((512, 256), 0), iota((512, 256), 1)
-    for half in range(2):
-        pick = jnp.where(
-            ((row // 8) * 4 + row % 4 == col) & ((row % 8) // 4 == half), 1.0, 0.0
-        ).astype(BF16)
-        at = slice(256 * half, 256 * half + 256)
-        big_hi[:, at] = mxu(pick, b_hi, ((1,), (1,))).astype(BF16)
-        big_lo[:, at] = mxu(pick, b_lo, ((1,), (1,))).astype(BF16)
-
-    most = pl.ds(0, 8 * (SEC - 1))
-    all_of(got_fibres.at[most], got_sem.at[0])
-    local1.wait()
-
-    x = got_fibres[...]
-    end = iota((8, 128), 1) == 127
-    codes = mxu(jnp.where(end, 1.0, 0.0).astype(BF16), x.astype(BF16), ((1,), (1,)))
-    slots = iota((8, 512), 1)
-    upper = slots % 8 >= 4
-    codes = jnp.where(upper, codes + 256.0, pltpu.roll(codes, 508, 1)) - 1.0
-    into_cells = jnp.where(iota((512, 512), 0).astype(F32) == codes[0:1], 1.0, 0.0).astype(BF16)
-    rows8 = iota((512, 128), 0) % 8
-    coded = (rows8 >= 4) & (iota((512, 128), 1) == 127)
-    x = jnp.where(coded, 0.0, x)
-    sums = jnp.sum(x, 1, keepdims=True)
-    sums = sums + pltpu.roll(jnp.broadcast_to(sums, (512, 128)), 4, 0)
-    x = jnp.where(coded, -sums, x)
-    x_hi, x_lo = split2(x)
-    cells = mxu(into_cells, x_hi) + mxu(into_cells, x_lo)
-
-    lanes = iota((64, 128), 1)
-    wide, odd = lanes >= 64, lanes % 64 >= 32
-    for half in range(2):
-        t = [cells[256 * half + 64 * a : 256 * half + 64 * a + 64] for a in range(4)]
-        for a in range(2):
-            p, q = t[a], t[a + 2]
-            t[a] = jnp.where(wide, pltpu.roll(q, 64, 1), p)
-            t[a + 2] = jnp.where(wide, q, pltpu.roll(p, 64, 1))
-        for a in (0, 2):
-            p, q = t[a], t[a + 1]
-            t[a] = jnp.where(odd, pltpu.roll(q, 32, 1), p)
-            t[a + 1] = jnp.where(odd, q, pltpu.roll(p, 96, 1))
-        for b in range(4):
-            slabs[4 * half + b] = t[b].reshape(2, 32, 128)
-
-    for i in range(1, RADN):
-        d = lax.rem(band + i, RADN)
-        pltpu.make_async_remote_copy(
-            slabs.at[d],
-            field.at[:, band],
-            send_sem.at[1],
-            got_sem.at[1],
-            device_id={"rad": d},
-            device_id_type=MESH,
-        ).start()
-    local2 = pltpu.make_async_copy(slabs.at[band], field.at[:, band], local_sem.at[1])
-    local2.start()
-    all_of(field.at[:, pl.ds(0, RADN - 1)], got_sem.at[1])
-    local2.wait()
-
-    f_hi, f_lo = split2(field[...].reshape(512, 128))
-    projected[...] = mxu(big_hi[...], f_hi) + mxu(big_hi[...], f_lo) + mxu(big_lo[...], f_hi)
-    local3 = over_sectors(projected, got_all, 2)
+    b_hi, b_lo = split2(basis[...].T)
+
+    all_of(codes_in.at[most], got_sem.at[0])
+    local_codes.wait()
+    codes = jnp.concatenate(
+        [
+            jnp.sum(codes_in[0:32, :], 0, keepdims=True),
+            jnp.sum(codes_in[32:64, :], 0, keepdims=True),
+        ],
+        1,
+    )
+    into_cells = jnp.where(iota((256, 256), 0).astype(F32) + 1.0 == codes, 1.0, 0.0).astype(BF16)
+
+    lanes = iota((32, 128), 1)
+
+    def deposit(c):
+        all_of(got_fibres.at[c, most4], got_sem.at[1 + c])
+        local_fibres[c].wait()
+        x_hi, x_lo = split2(got_fibres[c])
+        cells = mxu(into_cells, x_hi) + mxu(into_cells, x_lo)
+        t = [cells[32 * a : 32 * a + 32] for a in range(8)]
+        for step in (4, 2, 1):
+            width = 16 * step
+            late = lanes % (2 * width) >= width
+            for a in range(8):
+                if a // step % 2 == 0:
+                    p, q = t[a], t[a + step]
+                    t[a] = jnp.where(late, pltpu.roll(q, width, 1), p)
+                    t[a + step] = jnp.where(late, q, pltpu.roll(p, 128 - width, 1))
+        for q in range(8):
+            slabs[c, q // 2 + 4 * (q % 2)] = t[q]
+        for i in range(1, RADN):
+            d = lax.rem(band + i, RADN)
+            pltpu.make_async_remote_copy(
+                slabs.at[c, d],
+                field.at[c, band],
+                send_sem.at[3 + c],
+                got_sem.at[3 + c],
+                device_id={"rad": d},
+                device_id_type=MESH,
+            ).start()
+        local = pltpu.make_async_copy(slabs.at[c, band], field.at[c, band], local_sem.at[3 + c])
+        local.start()
+        return local
+
+    def project(c, local):
+        all_of(field.at[c, pl.ds(0, RADN - 1)], got_sem.at[3 + c])
+        local.wait()
+        f_hi, f_lo = split2(field[c].reshape(256, 128))
+        projected[c] = mxu(b_hi, f_hi) + mxu(b_hi, f_lo) + mxu(b_lo, f_hi)
+        return over_sectors(projected.at[c], got_all.at[c], 5 + c, 4)
+
+    last_copies = []
+    for c in range(2):
+        last_copies.append(project(c, deposit(c)))
+
     for c in stores:
         c.wait()
-    all_of(placed.at[most], send_sem.at[0])
-    all_of(slabs.at[pl.ds(0, RADN - 1)], send_sem.at[1])
-    all_of(got_all.at[most], got_sem.at[2])
-    local3.wait()
-    all_out[...] = got_all[...]
-    all_of(projected.at[most], send_sem.at[2])
+    all_of(codes_out.at[most], send_sem.at[0])
+    for c in range(2):
+        all_of(placed.at[c, most4], send_sem.at[1 + c])
+        all_of(slabs.at[c, pl.ds(0, RADN - 1)], send_sem.at[3 + c])
+    for c in range(2):
+        all_of(got_all.at[c, most4], got_sem.at[5 + c])
+        last_copies[c].wait()
+        all_out[c] = got_all[c]
+    for c in range(2):
+        all_of(projected.at[c, most4], send_sem.at[5 + c])
 
 
 def spectral_kernel(
@@ -339,9 +373,15 @@
     for c in passed:
         c.start()
     parts = []
+    near = iota((64, 128), 1) < 64
     for j in range(4):
-        z = all_ref[pl.ds(j, 128, stride=4), :].T
-        parts.append(jnp.concatenate([z[32 * a : 32 * a + 32] for a in range(4)], 1))
+        first, second = (all_ref[c, pl.ds(j, 64, stride=4), :] for c in range(2))
+        lower = jnp.where(near, first, pltpu.roll(second, 64, 1))
+        upper = jnp.where(near, pltpu.roll(first, 64, 1), second)
+        t = jnp.concatenate([lower, upper], 0).T
+        for c in range(2):
+            at = [64 * c + 16 * a for a in range(4)]
+            parts.append(jnp.concatenate([t[i : i + 16] for i in at], 1))
     hi, lo = split2(jnp.concatenate(parts, 0))
     for tile in range(4):
         at = slice(128 * tile, 128 * tile + 128)
@@ -357,8 +397,8 @@
 
 
 def azimuth_table():
-    low, rest = np.meshgrid(np.arange(4), np.arange(128), indexing="ij")
-    azimuth = (rest * 4 + low).reshape(-1)
+    low, high, sector = np.meshgrid(np.arange(4), np.arange(2), np.arange(SEC), indexing="ij")
+    azimuth = (sector * 8 + high * 4 + low).reshape(-1)
     phase = (azimuth[:, None] * np.arange(AZ)[None, :] % AZ) * (2.0 * math.pi / AZ)
     table = np.concatenate([np.cos(phase), -np.sin(phase)], 1) / math.sqrt(AZ)
     hi = table.astype(np.float32).astype(jnp.bfloat16)
@@ -380,51 +420,67 @@
 ):
     any_space = pl.BlockSpec(memory_space=pl.ANY)
     vmem = pl.BlockSpec(memory_space=pltpu.VMEM)
+    hbm = pl.BlockSpec(memory_space=pltpu.HBM)
     v_later, gates_later, everything = pl.pallas_call(
         exchange_kernel,
         out_shape=[
             jax.ShapeDtypeStruct((FIB, 256), F32),
             jax.ShapeDtypeStruct((3, FIB, 256), F32),
-            jax.ShapeDtypeStruct((512, 128), F32),
+            jax.ShapeDtypeStruct((2, 256, 128), F32),
         ],
-        in_specs=[any_space] * 3 + [vmem] * 6,
+        in_specs=[hbm] * 9,
         out_specs=[any_space, any_space, vmem],
         scratch_shapes=[
             pltpu.VMEM((FIB, 256), F32),
             pltpu.VMEM((3, FIB, 256), F32),
             pltpu.VMEM((256, 256), F32),
+            pltpu.VMEM((1, FIB), F32),
+            pltpu.VMEM((1, FIB), jnp.int32),
+            pltpu.VMEM((1, FIB), jnp.int32),
+            pltpu.VMEM((1, FIB), jnp.int32),
+            pltpu.VMEM((1, 512), jnp.int32),
+            pltpu.VMEM((1, FIB), jnp.int32),
             pltpu.VMEM((FIB, 256), F32),
             pltpu.VMEM((3, FIB, 256), F32),
             pltpu.VMEM((FIB, 128), F32),
-            pltpu.VMEM((2 * FIB, 128), F32),
-            pltpu.VMEM((512, 128), F32),
-            pltpu.VMEM((512, 128), F32),
-            pltpu.VMEM((512, 512), BF16),
-            pltpu.VMEM((512, 512), BF16),
-            pltpu.VMEM((8, 2, 32, 128), F32),
+            pltpu.VMEM((2, FIB, 128), F32),
+            pltpu.VMEM((SEC, 128), F32),
+            pltpu.VMEM((SEC, 128), F32),
+            pltpu.VMEM((2, 256, 128), F32),
+            pltpu.VMEM((2, 256, 128), F32),
             pltpu.VMEM((2, 8, 32, 128), F32),
-            pltpu.VMEM((512, 128), F32),
-            pltpu.VMEM((512, 128), F32),
+            pltpu.VMEM((2, 8, 32, 128), F32),
+            pltpu.VMEM((2, 256, 128), F32),
+            pltpu.VMEM((2, 256, 128), F32),
             pltpu.SemaphoreType.DMA((2,)),
+            pltpu.SemaphoreType.DMA((6,)),
             pltpu.SemaphoreType.DMA,
             pltpu.SemaphoreType.DMA((2,)),
-            pltpu.SemaphoreType.DMA((3,)),
-            pltpu.SemaphoreType.DMA((3,)),
-            pltpu.SemaphoreType.DMA((3,)),
+            pltpu.SemaphoreType.DMA((7,)),
+            pltpu.SemaphoreType.DMA((7,)),
+            pltpu.SemaphoreType.DMA((7,)),
         ],
         compiler_params=pltpu.CompilerParams(
             collective_id=0, has_side_effects=True, vmem_limit_bytes=32 << 20
         ),
+        cost_estimate=pl.CostEstimate(
+            flops=20_000_000_000, bytes_accessed=100_000_000, transcendentals=4_000_000
+        ),
     )(
-        voltage,
-        gates,
-        basis,
-        conductance.reshape(1, FIB),
-        sector_map.reshape(1, FIB),
-        cell_index.reshape(1, FIB),
-        neuron.reshape(1, FIB),
-        moment.reshape(1, 512),
-        synapse.reshape(1, FIB),
+        *(
+            pltpu.with_memory_space_constraint(a, pltpu.HBM)
+            for a in (
+                voltage,
+                gates,
+                basis,
+                conductance.reshape(1, FIB),
+                sector_map.reshape(1, FIB),
+                cell_index.reshape(1, FIB),
+                neuron.reshape(1, FIB),
+                moment.reshape(1, 512),
+                synapse.reshape(1, FIB),
+            )
+        )
     )
     table_hi, table_lo = azimuth_table()
     tiles, v_final, gates_final = pl.pallas_call(

time: 68.8 us -> 55.1 us (0.80)
  Pallas kernels: 61.8 us -> 54.3 us
  local copies, waits for them, and re-layouts: 5.98 us -> 0.02 us
    pallas_call x1, Pallas kernels: 59.9 us -> 52.3 us  [per_device(): pl.pallas_call(exchange_kernel, out_shape=[jax.ShapeDtypeStruct((FIB, 256...]
    unnamed x24 -> x6, local copies, waits for them, and re-layouts: 5.98 us -> 0.02 us
where the time goes in v2:
time: 55.1 us; the launch traced here: 55 us
  Pallas kernels  54.3 us (99%)
  between operations  0.69 us (1%)
    pallas_call x1, Pallas kernels, per_device(): pl.pallas_call(exchange_kernel, out_shape=[jax.ShapeDtypeStruct((FIB, 256...  52.3 us
    pallas_call x1, Pallas kernels, per_device(): pl.pallas_call(spectral_kernel, out_shape=[jax.ShapeDtypeStruct((1024, 12...  2 us

profile of v2, /device:TPU:1, one launch (start us, length us, event | category | flops | bytes accessed | tf_op | source)
XLA Modules:
  0.0 55.0 jit_solution(17588838149121582375)
XLA Ops:
  0.6 0.0 copy-start
  0.6 0.0 copy-start.1
  0.7 0.0 copy-start.2
  0.7 52.3 %shard_map.139 = (f32[128,256]{1,0:T(8,128)S(1)}, f32[3,128,256]{2,1,0:T(8,128)S(1)}, f32[2,256,128]{2,1,0:T(8,128)S(1)}) custom-call(f32[128,256]{1,0:T(8,128)} %v_hbm.1, f32[3,128,256]{2,1,0:T(8,128)} %gates_hbm.1, f32[256,256]{1,0:T(8,128)} %basis_hbm.1, f32[1,128]{1,0:T(1,128)} %bitcast.13, s32[1,128]{1,0:T(1,128)} %bitcast.14, s32[1,128]{1,0:T(1,128)} %bitcast.15, ...), custom_call_target="tpu_custom_call" | custom-call | flops 20000000000 | bytes 100000000 | tf_op jit(solution)/shard_map/pallas_call | solution.py:424
  53.0 0.0 copy-done
  53.0 0.0 copy-done.1
  53.0 0.0 copy-done.2
  53.0 2.0 %shard_map.140 = (f32[1024,128]{1,0:T(8,128)}, f32[128,256]{1,0:T(8,128)}, f32[3,128,256]{2,1,0:T(8,128)}) custom-call(f32[2,256,128]{2,1,0:T(8,128)S(1)} %get-tuple-element.9.all_ref, bf16[512,1024]{1,0:T(8,128)(2,1)S(1)} %copy-done.1, bf16[512,1024]{1,0:T(8,128)(2,1)S(1)} %copy-done, f32[4,512]{1,0:T(4,128)S(1)} %copy-done.2, ...), custom_call_target="tpu_custom_call" | custom-call | tf_op jit(solution)/shard_map/pallas_call | solution.py:486
Async XLA Ops:
  0.6 52.3 %copy-start = (bf16[512,1024]{1,0:T(8,128)(2,1)S(1)}, bf16[512,1024]{1,0:T(8,128)(2,1)}, u32[]{:S(2)}) copy-start(bf16[512,1024]{1,0:T(8,128)(2,1)} %constant.5.clone.table_lo) | copy-start | bytes 3145732
  0.6 52.3 %copy-start.1 = (bf16[512,1024]{1,0:T(8,128)(2,1)S(1)}, bf16[512,1024]{1,0:T(8,128)(2,1)}, u32[]{:S(2)}) copy-start(bf16[512,1024]{1,0:T(8,128)(2,1)} %constant.4.clone.table_hi) | copy-start | bytes 3145732
  0.7 52.3 %copy-start.2 = (f32[4,512]{1,0:T(4,128)S(1)}, f32[4,512]{1,0:T(4,128)}, u32[]{:S(2)}) copy-start(f32[4,512]{1,0:T(4,128)} %spectrum_ref.1) | copy-start | bytes 24580

commit v3 on v2

--- a/solution.py
+++ b/solution.py
@@ -158,13 +158,38 @@
 
     barrier = pltpu.get_barrier_semaphore()
 
-    def greet(i, carry):
-        pl.semaphore_signal(
-            barrier, inc=1, device_id={"sec": lax.rem(me + i, SEC)}, device_id_type=MESH
-        )
-        return carry
-
-    lax.fori_loop(1, SEC, greet, 0)
+    y, z = me // 16, lax.rem(me, 16)
+
+    def over_partners(act):
+        def far(i, carry):
+            away = 8 - (i + 1) // 2
+            to_z = lax.rem(z + jnp.where(lax.rem(i, 2) == 1, away, 16 - away), 16)
+            for to_y in (2, 1, 3, 0):
+                act(lax.rem(y + to_y, 4) * 16 + to_z)
+            return carry
+
+        lax.fori_loop(0, 15, far, 0)
+        for to_y in (2, 1, 3):
+            act(lax.rem(y + to_y, 4) * 16 + z)
+
+    def over_partners_in_order(act):
+        def at_z(to_z, carry):
+            for to_y in (2, 1, 3):
+                act(lax.rem(y + to_y, 4) * 16 + to_z)
+
+            @pl.when(to_z != z)
+            def _():
+                act(y * 16 + to_z)
+
+            return carry
+
+        lax.fori_loop(0, 16, at_z, 0)
+
+    over_partners(
+        lambda d: pl.semaphore_signal(
+            barrier, inc=1, device_id={"sec": d}, device_id_type=MESH
+        )
+    )
     for i in range(1, RADN):
         pl.semaphore_signal(
             barrier, inc=1, device_id={"rad": lax.rem(band + i, RADN)}, device_id_type=MESH
@@ -252,14 +277,10 @@
 
     pl.semaphore_wait(barrier, SEC + RADN - 2)
 
-    y, z = me // 16, lax.rem(me, 16)
-
-    def over_sectors(source, target, n, rows):
+    def over_sectors(source, target, n, rows, over=over_partners):
         own = pl.ds(pl.multiple_of(me * rows, rows), rows)
-
-        def send(to_y, to_z):
-            d = lax.rem(y + to_y, 4) * 16 + lax.rem(z + to_z, 16)
-            pltpu.make_async_remote_copy(
+        over(
+            lambda d: pltpu.make_async_remote_copy(
                 source.at[pl.ds(pl.multiple_of(d * rows, rows), rows)],
                 target.at[own],
                 send_sem.at[n],
@@ -267,17 +288,7 @@
                 device_id={"sec": d},
                 device_id_type=MESH,
             ).start()
-
-        def send_far(i, carry):
-            away = 8 - (i + 1) // 2
-            to_z = jnp.where(lax.rem(i, 2) == 1, away, 16 - away)
-            for to_y in (2, 1, 3, 0):
-                send(to_y, to_z)
-            return carry
-
-        lax.fori_loop(0, 15, send_far, 0)
-        for to_y in (2, 1, 3):
-            send(to_y, 0)
+        )
         local = pltpu.make_async_copy(source.at[own], target.at[own], local_sem.at[n])
         local.start()
         return local
@@ -288,12 +299,11 @@
     most = pl.ds(0, SEC - 1)
     most4 = pl.ds(0, 4 * (SEC - 1))
     local_codes = over_sectors(codes_out, codes_in, 0, 1)
-    local_fibres = [
-        over_sectors(placed.at[c], got_fibres.at[c], 1 + c, 4) for c in range(2)
-    ]
-
+    local_fibres = [over_sectors(placed.at[0], got_fibres.at[0], 1, 4)]
     load_basis.wait()
     b_hi, b_lo = split2(basis[...].T)
+    all_of(placed.at[0, most4], send_sem.at[1])
+    local_fibres.append(over_sectors(placed.at[1], got_fibres.at[1], 2, 4))
 
     all_of(codes_in.at[most], got_sem.at[0])
     local_codes.wait()
@@ -343,17 +353,21 @@
         local.wait()
         f_hi, f_lo = split2(field[c].reshape(256, 128))
         projected[c] = mxu(b_hi, f_hi) + mxu(b_hi, f_lo) + mxu(b_lo, f_hi)
-        return over_sectors(projected.at[c], got_all.at[c], 5 + c, 4)
+        return over_sectors(
+            projected.at[c], got_all.at[c], 5 + c, 4, over_partners_in_order if c else over_partners
+        )
 
     last_copies = []
+    deposits = [deposit(c) for c in range(2)]
     for c in range(2):
-        last_copies.append(project(c, deposit(c)))
+        last_copies.append(project(c, deposits[c]))
 
     for c in stores:
         c.wait()
     all_of(codes_out.at[most], send_sem.at[0])
     for c in range(2):
-        all_of(placed.at[c, most4], send_sem.at[1 + c])
+        if c == 1:
+            all_of(placed.at[c, most4], send_sem.at[1 + c])
         all_of(slabs.at[c, pl.ds(0, RADN - 1)], send_sem.at[3 + c])
     for c in range(2):
         all_of(got_all.at[c, most4], got_sem.at[5 + c])

time: 55.1 us -> 52 us (0.944)
  Pallas kernels: 54.3 us -> 51.2 us
    pallas_call x1, Pallas kernels: 52.3 us -> 49.2 us  [per_device(): pl.pallas_call(exchange_kernel, out_shape=[jax.ShapeDtypeStruct((FIB, 256...]
where the time goes in v3:
time: 52 us; the launch traced here: 51.9 us
  Pallas kernels  51.2 us (98%)
  between operations  0.69 us (1%)
    pallas_call x1, Pallas kernels, per_device(): pl.pallas_call(exchange_kernel, out_shape=[jax.ShapeDtypeStruct((FIB, 256...  49.2 us
    pallas_call x1, Pallas kernels, per_device(): pl.pallas_call(spectral_kernel, out_shape=[jax.ShapeDtypeStruct((1024, 12...  2 us

profile of v3, /device:TPU:1, one launch (start us, length us, event | category | flops | bytes accessed | tf_op | source)
XLA Modules:
  0.0 51.9 jit_solution(16358252564962877540)
XLA Ops:
  0.6 0.0 copy-start
  0.6 0.0 copy-start.1
  0.7 0.0 copy-start.2
  0.7 49.2 %shard_map.139 = (f32[128,256]{1,0:T(8,128)S(1)}, f32[3,128,256]{2,1,0:T(8,128)S(1)}, f32[2,256,128]{2,1,0:T(8,128)S(1)}) custom-call(f32[128,256]{1,0:T(8,128)} %v_hbm.1, f32[3,128,256]{2,1,0:T(8,128)} %gates_hbm.1, f32[256,256]{1,0:T(8,128)} %basis_hbm.1, f32[1,128]{1,0:T(1,128)} %bitcast.13, s32[1,128]{1,0:T(1,128)} %bitcast.14, s32[1,128]{1,0:T(1,128)} %bitcast.15, ...), custom_call_target="tpu_custom_call" | custom-call | flops 20000000000 | bytes 100000000 | tf_op jit(solution)/shard_map/pallas_call | solution.py:438
  49.8 0.0 copy-done
  49.8 0.0 copy-done.1
  49.8 0.0 copy-done.2
  49.9 2.0 %shard_map.140 = (f32[1024,128]{1,0:T(8,128)}, f32[128,256]{1,0:T(8,128)}, f32[3,128,256]{2,1,0:T(8,128)}) custom-call(f32[2,256,128]{2,1,0:T(8,128)S(1)} %get-tuple-element.9.all_ref, bf16[512,1024]{1,0:T(8,128)(2,1)S(1)} %copy-done.1, bf16[512,1024]{1,0:T(8,128)(2,1)S(1)} %copy-done, f32[4,512]{1,0:T(4,128)S(1)} %copy-done.2, ...), custom_call_target="tpu_custom_call" | custom-call | tf_op jit(solution)/shard_map/pallas_call | solution.py:500
Async XLA Ops:
  0.6 49.2 %copy-start = (bf16[512,1024]{1,0:T(8,128)(2,1)S(1)}, bf16[512,1024]{1,0:T(8,128)(2,1)}, u32[]{:S(2)}) copy-start(bf16[512,1024]{1,0:T(8,128)(2,1)} %constant.5.clone.table_lo) | copy-start | bytes 3145732
  0.6 49.2 %copy-start.1 = (bf16[512,1024]{1,0:T(8,128)(2,1)S(1)}, bf16[512,1024]{1,0:T(8,128)(2,1)}, u32[]{:S(2)}) copy-start(bf16[512,1024]{1,0:T(8,128)(2,1)} %constant.4.clone.table_hi) | copy-start | bytes 3145732
  0.7 49.2 %copy-start.2 = (f32[4,512]{1,0:T(4,128)S(1)}, f32[4,512]{1,0:T(4,128)}, u32[]{:S(2)}) copy-start(f32[4,512]{1,0:T(4,128)} %spectrum_ref.1) | copy-start | bytes 24580

commit v4 on v3

--- a/solution.py
+++ b/solution.py
@@ -132,6 +132,45 @@
     me = lax.axis_index("sec")
     band = lax.axis_index("rad")
 
+    barrier = pltpu.get_barrier_semaphore()
+
+    y, z = me // 16, lax.rem(me, 16)
+
+    def over_partners(act):
+        def far(i, carry):
+            away = 8 - (i + 1) // 2
+            to_z = lax.rem(z + jnp.where(lax.rem(i, 2) == 1, away, 16 - away), 16)
+            for to_y in (2, 1, 3, 0):
+                act(lax.rem(y + to_y, 4) * 16 + to_z)
+            return carry
+
+        lax.fori_loop(0, 15, far, 0)
+        for to_y in (2, 1, 3):
+            act(lax.rem(y + to_y, 4) * 16 + z)
+
+    def over_partners_in_order(act):
+        def at_z(to_z, carry):
+            for to_y in (2, 1, 3):
+                act(lax.rem(y + to_y, 4) * 16 + to_z)
+
+            @pl.when(to_z != z)
+            def _():
+                act(y * 16 + to_z)
+
+            return carry
+
+        lax.fori_loop(0, 16, at_z, 0)
+
+    over_partners(
+        lambda d: pl.semaphore_signal(
+            barrier, inc=1, device_id={"sec": d}, device_id_type=MESH
+        )
+    )
+    for i in range(1, RADN):
+        pl.semaphore_signal(
+            barrier, inc=1, device_id={"rad": lax.rem(band + i, RADN)}, device_id_type=MESH
+        )
+
     loads = [
         pltpu.make_async_copy(v_hbm, v_in, load_sem.at[0]),
         pltpu.make_async_copy(gates_hbm, gates_in, load_sem.at[1]),
@@ -155,45 +194,6 @@
         c.start()
     load_basis = pltpu.make_async_copy(basis_hbm, basis, basis_sem)
     load_basis.start()
-
-    barrier = pltpu.get_barrier_semaphore()
-
-    y, z = me // 16, lax.rem(me, 16)
-
-    def over_partners(act):
-        def far(i, carry):
-            away = 8 - (i + 1) // 2
-            to_z = lax.rem(z + jnp.where(lax.rem(i, 2) == 1, away, 16 - away), 16)
-            for to_y in (2, 1, 3, 0):
-                act(lax.rem(y + to_y, 4) * 16 + to_z)
-            return carry
-
-        lax.fori_loop(0, 15, far, 0)
-        for to_y in (2, 1, 3):
-            act(lax.rem(y + to_y, 4) * 16 + z)
-
-    def over_partners_in_order(act):
-        def at_z(to_z, carry):
-            for to_y in (2, 1, 3):
-                act(lax.rem(y + to_y, 4) * 16 + to_z)
-
-            @pl.when(to_z != z)
-            def _():
-                act(y * 16 + to_z)
-
-            return carry
-
-        lax.fori_loop(0, 16, at_z, 0)
-
-    over_partners(
-        lambda d: pl.semaphore_signal(
-            barrier, inc=1, device_id={"sec": d}, device_id_type=MESH
-        )
-    )
-    for i in range(1, RADN):
-        pl.semaphore_signal(
-            barrier, inc=1, device_id={"rad": lax.rem(band + i, RADN)}, device_id_type=MESH
-        )
 
     for c in small:
         c.wait()
@@ -334,7 +334,7 @@
                     t[a + step] = jnp.where(late, q, pltpu.roll(p, 128 - width, 1))
         for q in range(8):
             slabs[c, q // 2 + 4 * (q % 2)] = t[q]
-        for i in range(1, RADN):
+        for i in (4, 3, 5, 2, 6, 1, 7):
             d = lax.rem(band + i, RADN)
             pltpu.make_async_remote_copy(
                 slabs.at[c, d],
@@ -397,15 +397,19 @@
             at = [64 * c + 16 * a for a in range(4)]
             parts.append(jnp.concatenate([t[i : i + 16] for i in at], 1))
     hi, lo = split2(jnp.concatenate(parts, 0))
-    for tile in range(4):
-        at = slice(128 * tile, 128 * tile + 128)
+    for pair in range(2):
+        at = slice(256 * pair, 256 * pair + 256)
         scale = jnp.concatenate(
-            [jnp.broadcast_to(spectrum_ref[j : j + 1, at], (32, 128)) for j in range(4)], 0
+            [jnp.broadcast_to(spectrum_ref[j : j + 1, at], (32, 256)) for j in range(4)], 0
         )
         for part in range(2):
-            to = slice(512 * part + 128 * tile, 512 * part + 128 * tile + 128)
+            to = slice(512 * part + 256 * pair, 512 * part + 256 * pair + 256)
             y = mxu(hi, table_hi[:, to]) + mxu(lo, table_hi[:, to]) + mxu(hi, table_lo[:, to])
-            out_ref[pl.ds(2 * tile + part, 128, stride=8), :] = y * scale
+            y = y * scale
+            for tile in range(2):
+                out_ref[pl.ds(4 * pair + 2 * tile + part, 128, stride=8), :] = y[
+                    :, 128 * tile : 128 * tile + 128
+                ]
     for c in passed:
         c.wait()
 

time: 52 us -> 51.4 us (0.988)
  Pallas kernels: 51.2 us -> 50.5 us
where the time goes in v4:
time: 51.4 us; the launch traced here: 51.2 us
  Pallas kernels  50.5 us (98%)
  between operations  0.69 us (1%)
    pallas_call x1, Pallas kernels, per_device(): pl.pallas_call(exchange_kernel, out_shape=[jax.ShapeDtypeStruct((FIB, 256...  48.9 us
    pallas_call x1, Pallas kernels, per_device(): pl.pallas_call(spectral_kernel, out_shape=[jax.ShapeDtypeStruct((1024, 12...  1.62 us

profile of v4, /device:TPU:1, one launch (start us, length us, event | category | flops | bytes accessed | tf_op | source)
XLA Modules:
  0.0 51.2 jit_solution(13824426219650996877)
XLA Ops:
  0.6 0.0 copy-start
  0.6 0.0 copy-start.1
  0.7 0.0 copy-start.2
  0.7 48.9 %shard_map.139 = (f32[128,256]{1,0:T(8,128)S(1)}, f32[3,128,256]{2,1,0:T(8,128)S(1)}, f32[2,256,128]{2,1,0:T(8,128)S(1)}) custom-call(f32[128,256]{1,0:T(8,128)} %v_hbm.1, f32[3,128,256]{2,1,0:T(8,128)} %gates_hbm.1, f32[256,256]{1,0:T(8,128)} %basis_hbm.1, f32[1,128]{1,0:T(1,128)} %bitcast.13, s32[1,128]{1,0:T(1,128)} %bitcast.14, s32[1,128]{1,0:T(1,128)} %bitcast.15, ...), custom_call_target="tpu_custom_call" | custom-call | flops 20000000000 | bytes 100000000 | tf_op jit(solution)/shard_map/pallas_call | solution.py:442
  49.6 0.0 copy-done
  49.6 0.0 copy-done.1
  49.6 0.0 copy-done.2
  49.6 1.6 %shard_map.140 = (f32[1024,128]{1,0:T(8,128)}, f32[128,256]{1,0:T(8,128)}, f32[3,128,256]{2,1,0:T(8,128)}) custom-call(f32[2,256,128]{2,1,0:T(8,128)S(1)} %get-tuple-element.9.all_ref, bf16[512,1024]{1,0:T(8,128)(2,1)S(1)} %copy-done.1, bf16[512,1024]{1,0:T(8,128)(2,1)S(1)} %copy-done, f32[4,512]{1,0:T(4,128)S(1)} %copy-done.2, ...), custom_call_target="tpu_custom_call" | custom-call | tf_op jit(solution)/shard_map/pallas_call | solution.py:504
Async XLA Ops:
  0.6 49.0 %copy-start = (bf16[512,1024]{1,0:T(8,128)(2,1)S(1)}, bf16[512,1024]{1,0:T(8,128)(2,1)}, u32[]{:S(2)}) copy-start(bf16[512,1024]{1,0:T(8,128)(2,1)} %constant.5.clone.table_lo) | copy-start | bytes 3145732
  0.6 49.0 %copy-start.1 = (bf16[512,1024]{1,0:T(8,128)(2,1)S(1)}, bf16[512,1024]{1,0:T(8,128)(2,1)}, u32[]{:S(2)}) copy-start(bf16[512,1024]{1,0:T(8,128)(2,1)} %constant.4.clone.table_hi) | copy-start | bytes 3145732
  0.7 49.0 %copy-start.2 = (f32[4,512]{1,0:T(4,128)S(1)}, f32[4,512]{1,0:T(4,128)}, u32[]{:S(2)}) copy-start(f32[4,512]{1,0:T(4,128)} %spectrum_ref.1) | copy-start | bytes 24580

commit v5 on v4

--- a/solution.py
+++ b/solution.py
@@ -378,7 +378,7 @@
 
 
 def spectral_kernel(
-    all_ref, table_hi, table_lo, spectrum_ref, v_hbm, gates_hbm, out_ref, v_out, gates_out, sem
+    all_ref, table_hi, table_lo, spectrum_ref, v_hbm, gates_hbm, out_hbm, v_out, gates_out, tiles, sem
 ):
     passed = [
         pltpu.make_async_copy(v_hbm, v_out, sem.at[0]),
@@ -396,20 +396,27 @@
         for c in range(2):
             at = [64 * c + 16 * a for a in range(4)]
             parts.append(jnp.concatenate([t[i : i + 16] for i in at], 1))
-    hi, lo = split2(jnp.concatenate(parts, 0))
-    for pair in range(2):
-        at = slice(256 * pair, 256 * pair + 256)
-        scale = jnp.concatenate(
-            [jnp.broadcast_to(spectrum_ref[j : j + 1, at], (32, 256)) for j in range(4)], 0
-        )
-        for part in range(2):
-            to = slice(512 * part + 256 * pair, 512 * part + 256 * pair + 256)
-            y = mxu(hi, table_hi[:, to]) + mxu(lo, table_hi[:, to]) + mxu(hi, table_lo[:, to])
-            y = y * scale
-            for tile in range(2):
-                out_ref[pl.ds(4 * pair + 2 * tile + part, 128, stride=8), :] = y[
-                    :, 128 * tile : 128 * tile + 128
-                ]
+    for half in range(2):
+        hi, lo = split2(jnp.concatenate(parts[4 * half : 4 * half + 4], 0))
+        for pair in range(2):
+            at = slice(256 * pair, 256 * pair + 256)
+            scale = jnp.concatenate(
+                [
+                    jnp.broadcast_to(spectrum_ref[j : j + 1, at], (32, 256))
+                    for j in (2 * half, 2 * half + 1)
+                ],
+                0,
+            )
+            for part in range(2):
+                to = slice(512 * part + 256 * pair, 512 * part + 256 * pair + 256)
+                y = mxu(hi, table_hi[:, to]) + mxu(lo, table_hi[:, to]) + mxu(hi, table_lo[:, to])
+                y = y * scale
+                for tile in range(2):
+                    start = 512 * half + 4 * pair + 2 * tile + part
+                    tiles[pl.ds(start, 64, stride=8), :] = y[:, 128 * tile : 128 * tile + 128]
+        rows = pl.ds(512 * half, 512)
+        passed.append(pltpu.make_async_copy(tiles.at[rows], out_hbm.at[rows], sem.at[2 + half]))
+        passed[-1].start()
     for c in passed:
         c.wait()
 
@@ -509,8 +516,8 @@
             jax.ShapeDtypeStruct((3, FIB, 256), F32),
         ],
         in_specs=[vmem] * 4 + [any_space] * 2,
-        out_specs=[vmem, any_space, any_space],
-        scratch_shapes=[pltpu.SemaphoreType.DMA((2,))],
+        out_specs=[any_space] * 3,
+        scratch_shapes=[pltpu.VMEM((1024, 128), F32), pltpu.SemaphoreType.DMA((4,))],
         compiler_params=pltpu.CompilerParams(vmem_limit_bytes=32 << 20),
     )(
         everything,

time: 51.4 us -> 51.9 us (level)
  no operation moved by 1% of the time
where the time goes in v5:
time: 51.9 us; the launch traced here: 51.7 us
  Pallas kernels  51 us (98%)
  between operations  0.69 us (1%)
    pallas_call x1, Pallas kernels, per_device(): pl.pallas_call(exchange_kernel, out_shape=[jax.ShapeDtypeStruct((FIB, 256...  48.9 us
    pallas_call x1, Pallas kernels, per_device(): pl.pallas_call(spectral_kernel, out_shape=[jax.ShapeDtypeStruct((1024, 12...  2.08 us

profile of v5, /device:TPU:1, one launch (start us, length us, event | category | flops | bytes accessed | tf_op | source)
XLA Modules:
  0.0 51.7 jit_solution(14731605402334004490)
XLA Ops:
  0.6 0.0 copy-start
  0.6 0.0 copy-start.1
  0.7 0.0 copy-start.2
  0.7 48.9 %shard_map.139 = (f32[128,256]{1,0:T(8,128)S(1)}, f32[3,128,256]{2,1,0:T(8,128)S(1)}, f32[2,256,128]{2,1,0:T(8,128)S(1)}) custom-call(f32[128,256]{1,0:T(8,128)} %v_hbm.1, f32[3,128,256]{2,1,0:T(8,128)} %gates_hbm.1, f32[256,256]{1,0:T(8,128)} %basis_hbm.1, f32[1,128]{1,0:T(1,128)} %bitcast.13, s32[1,128]{1,0:T(1,128)} %bitcast.14, s32[1,128]{1,0:T(1,128)} %bitcast.15, ...), custom_call_target="tpu_custom_call" | custom-call | flops 20000000000 | bytes 100000000 | tf_op jit(solution)/shard_map/pallas_call | solution.py:449
  49.6 0.0 copy-done
  49.6 0.0 copy-done.1
  49.6 0.0 copy-done.2
  49.6 2.1 %shard_map.140 = (f32[1024,128]{1,0:T(8,128)}, f32[128,256]{1,0:T(8,128)}, f32[3,128,256]{2,1,0:T(8,128)}) custom-call(f32[2,256,128]{2,1,0:T(8,128)S(1)} %get-tuple-element.9.all_ref, bf16[512,1024]{1,0:T(8,128)(2,1)S(1)} %copy-done.1, bf16[512,1024]{1,0:T(8,128)(2,1)S(1)} %copy-done, f32[4,512]{1,0:T(4,128)S(1)} %copy-done.2, ...), custom_call_target="tpu_custom_call" | custom-call | tf_op jit(solution)/shard_map/pallas_call | solution.py:511
Async XLA Ops:
  0.6 49.0 %copy-start = (bf16[512,1024]{1,0:T(8,128)(2,1)S(1)}, bf16[512,1024]{1,0:T(8,128)(2,1)}, u32[]{:S(2)}) copy-start(bf16[512,1024]{1,0:T(8,128)(2,1)} %constant.5.clone.table_lo) | copy-start | bytes 3145732
  0.6 49.0 %copy-start.1 = (bf16[512,1024]{1,0:T(8,128)(2,1)S(1)}, bf16[512,1024]{1,0:T(8,128)(2,1)}, u32[]{:S(2)}) copy-start(bf16[512,1024]{1,0:T(8,128)(2,1)} %constant.4.clone.table_hi) | copy-start | bytes 3145732
  0.7 49.0 %copy-start.2 = (f32[4,512]{1,0:T(4,128)S(1)}, f32[4,512]{1,0:T(4,128)}, u32[]{:S(2)}) copy-start(f32[4,512]{1,0:T(4,128)} %spectrum_ref.1) | copy-start | bytes 24580
